TPU v7x, 512 devices: a whole 4x4x16 slice. The times are simulated.
512 devices in a mesh: grp: 16 (over z_hi, y, core), col: 32 (over z_lo, x).
Axes of the slice: x: 4, y: 4, z: 16 (z_hi: 2, z_lo: 8; z = z_hi * 8 + z_lo), core: 2. Of those that a mesh axis runs over, the one named last changes fastest.
Arguments:
- blocks: bfloat16 [8192, 320, 320], P(('grp', 'col')), may hold values from -0.3125 to 0.3125
- block_row: int32 [8192], P(('grp', 'col')), may hold values from 0 to 2047, as said below
- block_col: int32 [8192], P(('grp', 'col')), may hold values from 0 to 2047, as said below
- panel_owner: int32 [2], replicated, may hold values from 0 to 31, as said below
- basis: bfloat16 [2048, 320, 512], P(('grp', 'col')), may hold values from -0.1484375 to 0.1484375
Outputs:
- reduced: float32 [512, 2, 512], P('col')
Inputs may be any that keep to these rules, and one draw needn't show every extreme that they name: `block_row`: the blocks of device position d (blocks d * 16 onward) have row clusters among d * 4 to d * 4 + 3 and column clusters in the same row group; they come in 2 runs of 8 blocks, run s holding exactly the device's blocks of window step s (panel column panel_owner[s]); no two blocks of one device share both row and column cluster. `block_col`: see block_row. `panel_owner`: entries are distinct.
All inputs are finite; a program needn't handle non-finite values.
Results may differ from a plain program's by a relative error of at most 0.0029.
Values may be sent and summed in bfloat16 or wider, within the bound.
A program may use at most 64 MiB of HBM per device.

v0:
```python
import jax
import jax.numpy as jnp
from jax import lax
from jax.sharding import PartitionSpec as P


def spread(shard, axis, root):
    mine = lax.axis_index(axis) == root
    return lax.psum(jnp.where(mine, shard, jnp.zeros_like(shard)), axis)


def receive_panel(basis, panel_owner, window_step):
    return spread(basis, "col", panel_owner[window_step])


def gather_rows(weights, products):
    return jnp.einsum("rb,bim->rim", weights, products, precision=lax.Precision.HIGHEST).astype(
        jnp.bfloat16
    )


def local(blocks, block_row, block_col, panel_owner, basis):
    col_count = lax.axis_size("col")
    cluster_count = basis.shape[0]
    step_count = panel_owner.shape[0]
    block_count = blocks.shape[0]
    group_span = col_count * cluster_count
    local_row = block_row % cluster_count
    local_col = block_col % group_span
    panel_slot = local_col % cluster_count
    cluster_ids = jnp.arange(cluster_count, dtype=jnp.int32)
    row_onehot = (local_row[None, :] == cluster_ids[:, None]).astype(jnp.float32)
    run_length = block_count // step_count
    rows_list = []
    for window_step in range(step_count):
        first = window_step * run_length
        panel_now = receive_panel(basis, panel_owner, window_step)
        chosen = jnp.take(panel_now, panel_slot[first : first + run_length], axis=0)
        products = jnp.einsum(
            "bij,bjm->bim",
            blocks[first : first + run_length],
            chosen,
            preferred_element_type=jnp.float32,
        )
        rows_list.append(gather_rows(row_onehot[:, first : first + run_length], products))
    panel_rows = jnp.stack(rows_list)
    row_share = lax.psum_scatter(
        jnp.einsum("cik,scin->ksn", basis, panel_rows, preferred_element_type=jnp.float32),
        "col",
        scatter_dimension=0,
        tiled=True,
    )
    return lax.psum(row_share, "grp")


def solution(mesh):
    return jax.shard_map(
        local,
        mesh=mesh,
        in_specs=(
            P(("grp", "col"), None, None),
            P(("grp", "col")),
            P(("grp", "col")),
            P(),
            P(("grp", "col"), None, None),
        ),
        out_specs=P("col", None, None),
        check_vma=False,
    )
```

profile of v0, /device:TPU:1, one launch (start us, length us, event | category | flops | bytes accessed | tf_op | source)
XLA Modules:
  0.0 1216.6 jit_solution(2538000657105916264)
XLA Ops:
  6.5 0.0 all-reduce.10.cloned.1.call-start
  6.5 1.3 fusion.43
  9.2 0.0 copy-start.2
  9.2 0.0 copy-start.3
  9.2 3.0 broadcast_select_fusion.1
  12.2 0.0 all-reduce.10.cloned.1.call-update
  12.2 0.0 all-reduce.8.cloned.1.call-start
  12.3 0.0 copy-done.2
  12.3 0.1 compare_and_fusion.1
  12.4 0.0 copy-done.3
  12.4 444.9 %all-reduce.10.cloned.1.call-done = (bf16[4,320,512]{2,1,0:T(8,128)(2,1)}, bf16[4,320,512]{2,1,0:T(8,128)(2,1)}) async-done(((bf16[4,320,512]{2,1,0:T(8,128)(2,1)}, bf16[4,320,512]{2,1,0:T(8,128)(2,1)}), (bf16[4,320,512]{2,1,0:T(8,128)(2,1)}, bf16[4,320,512]{2,1,0:T(8,128)(2,1)})) %all-reduce.10.cloned.1.call-update) | async-done | bytes 2621456 | tf_op jit(solution)/shard_map/psum | solution.py:9
  457.3 2.0 gather_fusion
  459.3 3.1 fusion.10
  462.5 6.5 fusion.28
  469.0 2.0 gather_fusion.1
  471.0 3.2 fusion.8
  474.2 0.0 copy-start
  474.2 5.7 fusion.25
  479.8 0.0 copy-done
  479.8 0.0 copy-start.1
  479.8 1.9 pad_maximum_fusion
  481.7 0.0 copy-done.1
  481.7 1.6 fusion.16
  483.3 2.4 copy.9
  485.8 0.0 all-reduce.8.cloned.1.call-update
  485.8 0.0 all-reduce.6.cloned.1.call-start
  485.9 1.3 dynamic-slice
  487.8 455.3 %all-reduce.8.cloned.1.call-done = f32[512,2,512]{2,1,0:T(2,128)} async-done(((f32[512,2,512]{2,1,0:T(2,128)}), f32[512,2,512]{2,1,0:T(2,128)}) %all-reduce.8.cloned.1.call-update) | async-done | bytes 2097168
  943.1 1.5 constant_dynamic-slice_fusion
  944.5 0.0 all-reduce.6.cloned.1.call-update
  944.6 264.0 %all-reduce.6.cloned.1.call-done = f32[16,2,512]{2,1,0:T(2,128)} async-done(((f32[16,2,512]{2,1,0:T(2,128)}), f32[16,2,512]{2,1,0:T(2,128)}) %all-reduce.6.cloned.1.call-update) | async-done | bytes 65552 | tf_op jit(solution)/shard_map/psum | solution.py:53
  1208.6 1.5 copy.37
  (4 shorter events, 0.0 us)
Async XLA Ops:
  6.5 450.7 %all-reduce.10.cloned.1.call-start = ((), (), s32[]{:S(2)}) async-start(), calls=%async_computation.2 | async-start | bytes 5242880 | tf_op jit(solution)/shard_map/psum | solution.py:9
  9.2 3.1 copy-start.2
  9.2 3.2 copy-start.3
  12.2 930.8 %all-reduce.8.cloned.1.call-start = ((), (), s32[]{:S(2)}) async-start(), calls=%async_computation.1 | async-start | bytes 4194304
  474.2 5.7 copy-start
  479.8 1.9 copy-start.1
  485.8 722.8 %all-reduce.6.cloned.1.call-start = ((), (), s32[]{:S(2)}) async-start(), calls=%async_computation | async-start | bytes 131072 | tf_op jit(solution)/shard_map/psum | solution.py:53
Sparse Core Ops, SparseCore 0:
  12.3 444.8 all-reduce.9
  485.9 457.0 all-reduce.7
  946.2 262.2 all-reduce.5
where the time goes:
time: 1220 us
  waiting for transfers between devices  1160 us (95%)
  matrix products  20.1 us (2%)
  between operations  15.2 us (1%)
    unnamed x4, waiting for transfers between devices  455 us
    psum x1, waiting for transfers between devices, spread(): return lax.psum(jnp.where(mine, shard, jnp.zeros_like(shard)), axis)  445 us
    psum x1, waiting for transfers between devices, local(): return lax.psum(row_share, 'grp')  264 us
  transfers between devices with their start and end apart: 3, of which 3 were waited for; matrix products, arithmetic and copies ran while one was open for 0% of the time, Pallas kernels for 0%

commit v1 on v0

v1 whole, which is shorter than its diff:
```python
import jax
import jax.numpy as jnp
from jax import lax
from jax.experimental import pallas as pl
from jax.experimental.pallas import tpu as pltpu
from jax.sharding import PartitionSpec as P

X, Y, Z, ZH, CORES = 4, 4, 8, 2, 2
RING = Z * ZH
BS, MODES, STEPS, CL, RUN = 320, 512, 2, 4, 8
PAD = 384
CHUNKS = 10
CH = BS // CHUNKS
PIECES = 10
PC = BS // PIECES
PH = PC // 2
T = STEPS * CHUNKS
G = STEPS * PIECES
SKEW = 3
AHEAD = 4
LEAD = 3
LAG = 3
COLS = X * Z
NH = 2
BF, F32 = jnp.bfloat16, jnp.float32


class Here:
    def __init__(self):
        grp, col = lax.axis_index("grp"), lax.axis_index("col")
        self.core, self.y, self.zh = grp % CORES, (grp // CORES) % Y, grp // (CORES * Y)
        self.z, self.x = col // X, col % X
        self.zg = self.zh * Z + self.z

    def at(self, zh=None, y=None, core=None, z=None, x=None):
        zh = self.zh if zh is None else zh
        y = self.y if y is None else y
        core = self.core if core is None else core
        z = self.z if z is None else z
        x = self.x if x is None else x
        return ((zh * Y + y) * CORES + core, z * X + x)

    def ring(self, d):
        p = (self.zg + d) % RING
        return self.at(zh=p // Z, z=p % Z)


def send(src, dst, ssem, rsem, dev):
    pltpu.make_async_remote_copy(
        src_ref=src, dst_ref=dst, send_sem=ssem, recv_sem=rsem,
        device_id=dev, device_id_type=pl.DeviceIdType.MESH,
    ).start()


def drain(ref, sem):
    pltpu.make_async_copy(ref, ref, sem).wait()


def meet(peers):
    barrier = pltpu.get_barrier_semaphore()
    for dev in peers:
        pl.semaphore_signal(barrier, inc=1, device_id=dev, device_id_type=pl.DeviceIdType.MESH)
    pl.semaphore_wait(barrier, len(peers))


def body(
    owner, brow, bcol, basis, blocks, out,
    blk, dense, basis_t, tsp, got, tr, tl, up_in, dn_in, up_out, dn_out, pan,
    share, core_in, mine, theirs, b3, z_in, out_all,
    blk_sem, s_x, s_tr, s_rl, s_z, s_ag, s_fw, s_core, s_p, s_zz, s_out,
    r_right, r_left, r_tr, r_tl, r_fr, r_fl, r_up, r_dn, r_ar, r_al, r_br, r_bl,
    r_core, r_p, r_zz, r_out,
):
    here = Here()
    core, x, y, z, zh, zg, at, ring = here.core, here.x, here.y, here.z, here.zh, here.zg, here.at, here.ring
    xr, xl, xo = (x + 1) % X, (x + 3) % X, (x + 2) % X
    right, left = at(x=xr), at(x=xl)
    above, below = at(z=(z + 1) % Z), at(z=(z + Z - 1) % Z)
    plane = [(dx, dy) for dx in range(X) for dy in range(Y) if dx or dy]
    copies = [(dh, dy, dc) for dh in range(ZH) for dy in range(Y) for dc in range(CORES) if dh or dy or dc]

    fetch = pltpu.make_async_copy(blocks, blk, blk_sem)
    fetch.start()

    def copy_at(dh, dy, dc):
        return (zh + dh) % ZH, (y + dy) % Y, (core + dc) % CORES

    peers = [at(x=(x + dx) % X, y=(y + dy) % Y) for dx, dy in plane]
    peers += [ring(d) for d in range(1, RING)]
    for dh, dy, dc in copies:
        if dc or (dh and dy):
            hh, yy, cc = copy_at(dh, dy, dc)
            peers.append(at(zh=hh, y=yy, core=cc))
    meet(peers)

    def piece(k):
        start = k * PC
        return (
            pl.ds(pl.multiple_of(start, PC), PC),
            pl.ds(pl.multiple_of(start, PH), PH),
            pl.ds(pl.multiple_of(start + PH, PH), PH),
            pl.ds(pl.multiple_of(k * PH, PH), PH),
        )

    def offer(k):
        rows, first, second, half = piece(k)
        send(basis.at[xo, first], tr.at[half], s_tr.at[0], r_tr.at[k], right)
        send(basis.at[xo, second], tl.at[half], s_tr.at[1], r_tl.at[k], left)
        send(basis.at[xr, rows], got.at[3, rows], s_x.at[0], r_right.at[k], right)
        send(basis.at[xl, rows], got.at[1, rows], s_x.at[1], r_left.at[k], left)

    for k in range(AHEAD):
        offer(k)
    got[0] = basis[x]
    for c in range(CL):
        pads = slice(c * PAD + BS, (c + 1) * PAD)
        basis_t[:, pads] = jnp.zeros((MODES, PAD - BS), BF)
        for s in range(STEPS):
            pan[s, c, BS:] = jnp.zeros((PAD - BS, MODES), BF)
            tsp[s, pads] = jnp.zeros((PAD - BS, MODES), BF)
            dense[s, :, pads] = jnp.zeros((CL * BS, PAD - BS), BF)

    def turn(i):
        c, m = i // CL, i % CL
        lanes = pl.ds(pl.multiple_of(m * 128, 128), 128)
        piece = basis[c, :, lanes].astype(F32).T.astype(BF)
        basis_t[lanes, pl.ds(pl.multiple_of(c * PAD, PAD), BS)] = piece

    def place(i):
        s, r, c = i // (CL * CL), (i // CL) % CL, i % CL
        where, found = jnp.int32(0), jnp.int32(0)
        for b in range(RUN):
            hit = (brow[s * RUN + b] % CL == r) & (bcol[s * RUN + b] % CL == c)
            where = jnp.where(hit, b, where)
            found = jnp.where(hit, 1, found)
        one = blk[s * RUN + where]
        one = jnp.where(found > 0, one, jnp.zeros_like(one))
        dense[s, pl.ds(pl.multiple_of(r * BS, BS), BS), pl.ds(pl.multiple_of(c * PAD, PAD), BS)] = one

    fetch.wait()

    owner_x = [owner[s] % X for s in range(STEPS)]
    owner_z = [owner[s] // X for s in range(STEPS)]
    far = jnp.maximum(z, Z - 1 - z)

    def pick(s, values):
        return jnp.where(s == 0, values[0], values[1])

    reach = LEAD + SKEW * far

    @pl.loop(0, LEAD + SKEW * (Z - 1) + T + LAG)
    def _(slot):
        @pl.when(slot < PIECES)
        def _():
            rows, first, second, half = piece(slot)
            drain(tr.at[half], r_tr.at[slot])
            send(tr.at[half], got.at[2, first], s_rl.at[0], r_fr.at[slot], right)
            drain(tl.at[half], r_tl.at[slot])
            send(tl.at[half], got.at[2, second], s_rl.at[1], r_fl.at[slot], left)

        @pl.when(slot < PIECES - AHEAD)
        def _():
            offer(slot + AHEAD)

        tg = slot - LEAD
        @pl.when((tg >= 0) & (tg < PIECES))
        def _():
            rows, first, second, half = piece(tg)
            drain(got.at[3, rows], r_right.at[tg])
            drain(got.at[1, rows], r_left.at[tg])
            drain(got.at[2, first], r_fr.at[tg])
            drain(got.at[2, second], r_fl.at[tg])

        def stream(t, inn, outt, rsem, ssem, has_in, has_out, dev):
            s, k = t // CHUNKS, t % CHUNKS
            rows = pl.ds(pl.multiple_of(k * CH, CH), CH)
            gap = (pick(s, owner_x) + X - x) % X
            own = got[0, rows]
            for d in range(1, X):
                own = jnp.where(gap == d, got[d, rows], own)

            @pl.when(has_in)
            def _():
                drain(inn.at[s, rows], rsem.at[t])
                outt[s, rows] = jnp.where(pick(s, owner_z) == z, own, inn[s, rows])

            @pl.when(jnp.logical_not(has_in))
            def _():
                outt[s, rows] = own

            @pl.when(has_out)
            def _():
                send(outt.at[s, rows], inn.at[s, rows], ssem, rsem.at[t], dev)

        tu = slot - LEAD - SKEW * z
        @pl.when((tu >= 0) & (tu < T))
        def _():
            stream(tu, up_in, up_out, r_up, s_z.at[0], z > 0, z < Z - 1, above)

        td = slot - LEAD - SKEW * (Z - 1 - z)
        @pl.when((td >= 0) & (td < T))
        def _():
            stream(td, dn_in, dn_out, r_dn, s_z.at[1], z < Z - 1, z > 0, below)

        tq = slot - reach
        @pl.when((tq >= 0) & (tq < T))
        def _():
            s, k = tq // CHUNKS, tq % CHUNKS
            rows = pl.ds(pl.multiple_of(k * CH, CH), CH)
            pan[s, x, rows] = jnp.where(pick(s, owner_z) <= z, up_out[s, rows], dn_out[s, rows])

            send(pan.at[s, x, rows], pan.at[s, x, rows], s_ag.at[0], r_ar.at[tq], right)
            send(pan.at[s, x, rows], pan.at[s, x, rows], s_ag.at[1], r_al.at[tq], left)

        tf = slot - reach - LAG
        @pl.when((tf >= 0) & (tf < T))
        def _():
            s = tf // PIECES
            rows, first, second, half = piece(tf % PIECES)
            drain(pan.at[s, xl, rows], r_ar.at[tf])
            send(pan.at[s, xl, first], pan.at[s, xl, first], s_fw.at[0], r_br.at[tf], right)
            drain(pan.at[s, xr, rows], r_al.at[tf])
            send(pan.at[s, xr, second], pan.at[s, xr, second], s_fw.at[1], r_bl.at[tf], left)

        @pl.when(slot < CL * CL)
        def _():
            turn(slot)

        @pl.when(slot < STEPS * CL * CL)
        def _():
            place(slot)

    def wait_panel(s):
        for k in range(PIECES):
            drain(pan.at[s, xo, k * PC : k * PC + PH], r_br.at[s * PIECES + k])
            drain(pan.at[s, xo, k * PC + PH : (k + 1) * PC], r_bl.at[s * PIECES + k])

    def panel_rows(s, n):
        lanes = slice(n * 256, (n + 1) * 256)
        rows = jnp.dot(
            dense[s], pan[s].reshape(CL * PAD, MODES)[:, lanes], preferred_element_type=F32
        ).astype(BF)
        for r in range(CL):
            tsp[s, r * PAD : r * PAD + BS, lanes] = rows[r * BS : (r + 1) * BS]

    def project(s, n):
        part = jnp.dot(
            basis_t[...], tsp[s, :, n * 256 : (n + 1) * 256], preferred_element_type=F32
        ).reshape(COLS, CORES, 8, 256)
        for k in range(CORES):
            share[k, s, n] = part[:, k]
        send(share.at[1 - core, s, n], core_in.at[s, n], s_core.at[s, n], r_core.at[s, n], at(core=1 - core))

    def over_plane(s):
        for n in range(NH):
            drain(core_in.at[s, n], r_core.at[s, n])
            for i in range(X):
                both = jnp.concatenate(
                    [share[core, s, n, zz * X + i] + core_in[s, n, zz * X + i] for zz in range(Z)], axis=0
                ).astype(BF)
                for j in range(2):
                    mine[s, i, n * 2 + j] = both[:, j * 128 : (j + 1) * 128]
        for i, (dx, dy) in enumerate(plane):
            xx, yy = (x + dx) % X, (y + dy) % Y
            send(mine.at[s, xx, yy], theirs.at[s, x, y], s_p.at[s, i], r_p.at[s, x * Y + y], at(x=xx, y=yy))

    def over_z():
        for s in range(STEPS):
            total = mine[s, x, y].astype(F32)
            for dx, dy in plane:
                xx, yy = (x + dx) % X, (y + dy) % Y
                drain(theirs.at[s, xx, yy], r_p.at[s, xx * Y + yy])
                total += theirs[s, xx, yy].astype(F32)
            for zz in range(Z):
                b3[s, zz] = total[zz * 8 : (zz + 1) * 8]
        for d in range(1, RING):
            p = (zg + d) % RING
            send(b3.at[p // Z, p % Z], z_in.at[zg], s_zz.at[d - 1], r_zz.at[zg], ring(d))
        z_in[zg] = b3[zh, z]

    def spread():
        for d in range(1, RING):
            p = (zg + d) % RING
            drain(z_in.at[p], r_zz.at[p])
        total = z_in[0]
        for p in range(1, RING):
            total += z_in[p]
        out_all[zh, y, core] = total
        for i, (dh, dy, dc) in enumerate(copies):
            hh, yy, cc = copy_at(dh, dy, dc)
            send(
                out_all.at[zh, y, core], out_all.at[zh, y, core], s_out.at[i],
                r_out.at[(zh * Y + y) * CORES + core], at(zh=hh, y=yy, core=cc),
            )

    def finish():
        for dh, dy, dc in copies:
            hh, yy, cc = copy_at(dh, dy, dc)
            drain(out_all.at[hh, yy, cc], r_out.at[(hh * Y + yy) * CORES + cc])
        for s in range(STEPS):
            for k in range(CORES):
                for j in range(Y):
                    out[s, k * 8 : (k + 1) * 8, j * 128 : (j + 1) * 128] = out_all[s, j, k]

    wait_panel(0)
    panel_rows(0, 0)
    panel_rows(0, 1)
    project(0, 0)
    project(0, 1)
    wait_panel(1)
    panel_rows(1, 0)
    over_plane(0)
    panel_rows(1, 1)
    project(1, 0)
    project(1, 1)
    over_plane(1)
    over_z()
    spread()
    finish()

    drain(basis.at[xr], s_x.at[0])
    drain(basis.at[xl], s_x.at[1])
    drain(tr, s_tr.at[0])
    drain(tl, s_tr.at[1])
    drain(tr, s_rl.at[0])
    drain(tl, s_rl.at[1])

    @pl.when(z < Z - 1)
    def _():
        drain(up_out, s_z.at[0])

    @pl.when(z > 0)
    def _():
        drain(dn_out, s_z.at[1])

    for i in range(2):
        drain(up_out, s_ag.at[i])
        drain(up_out.at[0], s_fw.at[i])
    for s in range(STEPS):
        for n in range(NH):
            drain(core_in.at[s, n], s_core.at[s, n])
        for i in range(len(plane)):
            drain(mine.at[s, 0, 0], s_p.at[s, i])
    for d in range(RING - 1):
        drain(z_in.at[0], s_zz.at[d])
    for i in range(len(copies)):
        drain(z_in.at[0], s_out.at[i])


def local(blocks, block_row, block_col, panel_owner, basis):
    dma = pltpu.SemaphoreType.DMA
    vmem = pltpu.VMEM
    scratch = [
        vmem((STEPS * RUN, BS, BS), BF),
        vmem((STEPS, CL * BS, CL * PAD), BF),
        vmem((MODES, CL * PAD), BF),
        vmem((STEPS, CL * PAD, MODES), BF),
        vmem((X, BS, MODES), BF),
        vmem((BS // 2, MODES), BF),
        vmem((BS // 2, MODES), BF),
        vmem((STEPS, BS, MODES), BF),
        vmem((STEPS, BS, MODES), BF),
        vmem((STEPS, BS, MODES), BF),
        vmem((STEPS, BS, MODES), BF),
        vmem((STEPS, CL, PAD, MODES), BF),
        vmem((CORES, STEPS, NH, COLS, 8, 256), F32),
        vmem((STEPS, NH, COLS, 8, 256), F32),
        vmem((STEPS, X, Y, 8 * Z, 128), BF),
        vmem((STEPS, X, Y, 8 * Z, 128), BF),
        vmem((STEPS, Z, 8, 128), F32),
        vmem((RING, 8, 128), F32),
        vmem((STEPS, Y, CORES, 8, 128), F32),
        dma, dma((2,)), dma((2,)), dma((2,)), dma((2,)), dma((2,)), dma((2,)),
        dma((STEPS, NH)), dma((STEPS, X * Y - 1)), dma((RING - 1,)), dma((ZH * Y * CORES - 1,)),
        dma((PIECES,)), dma((PIECES,)), dma((PIECES,)), dma((PIECES,)), dma((PIECES,)), dma((PIECES,)),
        dma((T,)), dma((T,)), dma((G,)), dma((G,)), dma((G,)), dma((G,)),
        dma((STEPS, NH)), dma((STEPS, X * Y)), dma((RING,)), dma((ZH * Y * CORES,)),
    ]
    smem = pl.BlockSpec(memory_space=pltpu.SMEM)
    whole = pl.BlockSpec(memory_space=pltpu.VMEM)
    result = pl.pallas_call(
        body,
        out_shape=jax.ShapeDtypeStruct((STEPS, CORES * 8, MODES), F32),
        in_specs=[smem, smem, smem, whole, pl.BlockSpec(memory_space=pl.ANY)],
        out_specs=whole,
        scratch_shapes=scratch,
        compiler_params=pltpu.CompilerParams(
            collective_id=0, has_side_effects=True, vmem_limit_bytes=56 * 1024 * 1024
        ),
        cost_estimate=pl.CostEstimate(flops=4_000_000_000, bytes_accessed=5_000_000, transcendentals=0),
        name="galerkin",
    )(panel_owner, block_row, block_col, basis, blocks)
    return jnp.transpose(result, (1, 0, 2))


def solution(mesh):
    return jax.shard_map(
        local,
        mesh=mesh,
        in_specs=(
            P(("grp", "col"), None, None),
            P(("grp", "col")),
            P(("grp", "col")),
            P(),
            P(("grp", "col"), None, None),
        ),
        out_specs=P("col", None, None),
        check_vma=False,
    )
```

time: 1220 us -> 116 us (0.10)
  waiting for transfers between devices: 1160 us -> 0 us
  Pallas kernels: 0 us -> 115 us
  matrix products: 20.1 us -> 0 us
  between operations: 15.2 us -> 0.01 us
    psum x2 -> x0, waiting for transfers between devices: 709 us -> none  [the longest x1 445 us: spread(): return lax.psum(jnp.where(mine, shard, jnp.zeros_like(shard)), axis)]
    unnamed x4 -> x0, waiting for transfers between devices: 455 us -> none
    pallas_call x0 -> x1, Pallas kernels: none -> 115 us  [local(): pl.pallas_call(body, out_shape=jax.ShapeDtypeStruct((STEPS, CORES * 8, MO...]
    dot_general x5 -> x0, matrix products: 20.1 us -> none  [the longest x2 12.1 us: gather_rows(): jnp.einsum('rb,bim->rim', weights, products, precision=lax.Precision.HIGH...]
  transfers between devices with their start and end apart: 3 -> 0, of which waited for: 3 -> 0; matrix products, arithmetic and copies ran while one was open for 0% -> 0% of each run, Pallas kernels for 0% -> 0%
where the time goes in v1:
time: 116 us
  Pallas kernels  115 us (99%)
  local copies, waits for them, and re-layouts  1.52 us (1%)
    pallas_call x1, Pallas kernels, local(): pl.pallas_call(body, out_shape=jax.ShapeDtypeStruct((STEPS, CORES * 8, MO...  115 us

profile of v1, /device:TPU:1, one launch (start us, length us, event | category | flops | bytes accessed | tf_op | source)
XLA Modules:
  0.0 116.0 jit_solution(8386032532291446518)
XLA Ops:
  0.0 114.5 %galerkin.1 = f32[2,16,512]{2,1,0:T(8,128)} custom-call(s32[2]{0:T(128)} %owner.1, s32[16]{0:T(128)} %brow.1, s32[16]{0:T(128)} %bcol.1, bf16[4,320,512]{2,1,0:T(8,128)(2,1)} %basis.1, bf16[16,320,320]{2,1,0:T(8,128)(2,1)} %blocks.1), custom_call_target="tpu_custom_call" | custom-call | flops 4000000000 | bytes 5000000 | tf_op jit(solution)/shard_map/galerkin/pallas_call | solution.py:381
  114.5 1.5 %copy.6 = f32[16,2,512]{2,1,0:T(2,128)} copy(f32[16,2,512]{2,0,1:T(8,128)} %bitcast.1) | data formatting | bytes 131072 | tf_op jit(solution)/shard_map/transpose | solution.py:393

commit v2 on v1

--- a/solution.py
+++ b/solution.py
@@ -9,6 +9,7 @@
 RING = Z * ZH
 BS, MODES, STEPS, CL, RUN = 320, 512, 2, 4, 8
 PAD = 384
+W2 = STEPS * BS
 CHUNKS = 10
 CH = BS // CHUNKS
 PIECES = 10
@@ -19,7 +20,12 @@
 SKEW = 3
 AHEAD = 4
 LEAD = 3
-LAG = 3
+WP = 8
+WR = MODES // WP
+HM = MODES // CORES
+W_AT = 8
+W_GO, W_STEP = 11, 2
+W_SUM = 36
 COLS = X * Z
 NH = 2
 BF, F32 = jnp.bfloat16, jnp.float32
@@ -65,16 +71,16 @@
 
 def body(
     owner, brow, bcol, basis, blocks, out,
-    blk, dense, basis_t, tsp, got, tr, tl, up_in, dn_in, up_out, dn_out, pan,
-    share, core_in, mine, theirs, b3, z_in, out_all,
-    blk_sem, s_x, s_tr, s_rl, s_z, s_ag, s_fw, s_core, s_p, s_zz, s_out,
-    r_right, r_left, r_tr, r_tl, r_fr, r_fl, r_up, r_dn, r_ar, r_al, r_br, r_bl,
-    r_core, r_p, r_zz, r_out,
+    blk, dense, basis_t, w_own, w_out, w_in, w_sum, w_pass,
+    got, tr, tl, up_in, dn_in, up_out, dn_out, q,
+    mine, kept, theirs, b3, z_in, out_all,
+    blk_sem, s_x, s_tr, s_rl, s_z, s_w, s_c, s_q, s_p, s_zz, s_out,
+    r_right, r_left, r_tr, r_tl, r_fr, r_fl, r_up, r_dn, r_w, r_c, r_q, r_p, r_zz, r_out,
 ):
     here = Here()
     core, x, y, z, zh, zg, at, ring = here.core, here.x, here.y, here.z, here.zh, here.zg, here.at, here.ring
     xr, xl, xo = (x + 1) % X, (x + 3) % X, (x + 2) % X
-    right, left = at(x=xr), at(x=xl)
+    right, left, other = at(x=xr), at(x=xl), at(core=1 - core)
     above, below = at(z=(z + 1) % Z), at(z=(z + Z - 1) % Z)
     plane = [(dx, dy) for dx in range(X) for dy in range(Y) if dx or dy]
     copies = [(dh, dy, dc) for dh in range(ZH) for dy in range(Y) for dc in range(CORES) if dh or dy or dc]
@@ -112,22 +118,18 @@
     for k in range(AHEAD):
         offer(k)
     got[0] = basis[x]
-    for c in range(CL):
-        pads = slice(c * PAD + BS, (c + 1) * PAD)
-        basis_t[:, pads] = jnp.zeros((MODES, PAD - BS), BF)
-        for s in range(STEPS):
-            pan[s, c, BS:] = jnp.zeros((PAD - BS, MODES), BF)
-            tsp[s, pads] = jnp.zeros((PAD - BS, MODES), BF)
-            dense[s, :, pads] = jnp.zeros((CL * BS, PAD - BS), BF)
-
-    def turn(i):
-        c, m = i // CL, i % CL
+    for g in range(CORES):
+        q[g, 0, BS:] = jnp.zeros((PAD - BS, MODES), BF)
+        q[g, 1, : PAD - BS] = jnp.zeros((PAD - BS, MODES), BF)
+
+    def turn(m):
         lanes = pl.ds(pl.multiple_of(m * 128, 128), 128)
-        piece = basis[c, :, lanes].astype(F32).T.astype(BF)
-        basis_t[lanes, pl.ds(pl.multiple_of(c * PAD, PAD), BS)] = piece
-
-    def place(i):
-        s, r, c = i // (CL * CL), (i // CL) % CL, i % CL
+        flipped = basis[:, :, lanes].reshape(CL * BS, 128).astype(F32).T.reshape(8, CORES, 8, CL * BS)
+        for k in range(CORES):
+            rows = pl.ds(pl.multiple_of(k * HM + m * 64, 64), 64)
+            basis_t[rows] = flipped[:, k].reshape(64, CL * BS).astype(BF)
+
+    def place(s, r, c):
         where, found = jnp.int32(0), jnp.int32(0)
         for b in range(RUN):
             hit = (brow[s * RUN + b] % CL == r) & (bcol[s * RUN + b] % CL == c)
@@ -135,7 +137,10 @@
             found = jnp.where(hit, 1, found)
         one = blk[s * RUN + where]
         one = jnp.where(found > 0, one, jnp.zeros_like(one))
-        dense[s, pl.ds(pl.multiple_of(r * BS, BS), BS), pl.ds(pl.multiple_of(c * PAD, PAD), BS)] = one
+        dense[c, pl.ds(pl.multiple_of(r * BS, BS), BS), s * BS : (s + 1) * BS] = one
+
+    def multiply(c):
+        return jnp.dot(basis_t[...], dense[c], preferred_element_type=F32)
 
     fetch.wait()
 
@@ -148,7 +153,7 @@
 
     reach = LEAD + SKEW * far
 
-    @pl.loop(0, LEAD + SKEW * (Z - 1) + T + LAG)
+    @pl.loop(0, LEAD + SKEW * (Z - 1) + T)
     def _(slot):
         @pl.when(slot < PIECES)
         def _():
@@ -207,66 +212,94 @@
         def _():
             s, k = tq // CHUNKS, tq % CHUNKS
             rows = pl.ds(pl.multiple_of(k * CH, CH), CH)
-            pan[s, x, rows] = jnp.where(pick(s, owner_z) <= z, up_out[s, rows], dn_out[s, rows])
-
-            send(pan.at[s, x, rows], pan.at[s, x, rows], s_ag.at[0], r_ar.at[tq], right)
-            send(pan.at[s, x, rows], pan.at[s, x, rows], s_ag.at[1], r_al.at[tq], left)
-
-        tf = slot - reach - LAG
-        @pl.when((tf >= 0) & (tf < T))
-        def _():
-            s = tf // PIECES
-            rows, first, second, half = piece(tf % PIECES)
-            drain(pan.at[s, xl, rows], r_ar.at[tf])
-            send(pan.at[s, xl, first], pan.at[s, xl, first], s_fw.at[0], r_br.at[tf], right)
-            drain(pan.at[s, xr, rows], r_al.at[tf])
-            send(pan.at[s, xr, second], pan.at[s, xr, second], s_fw.at[1], r_bl.at[tf], left)
-
-        @pl.when(slot < CL * CL)
+            here_rows = pl.ds(pl.multiple_of(s * (PAD - BS) + k * CH, CH), CH)
+            q[core, s, here_rows] = jnp.where(pick(s, owner_z) <= z, up_out[s, rows], dn_out[s, rows])
+
+
+            send(q.at[core, s, here_rows], q.at[core, s, here_rows], s_q, r_q.at[s], other)
+
+        tw = slot - W_GO
+        @pl.when((tw >= 0) & (tw % W_STEP == 0) & (tw < WP * W_STEP))
+        def _():
+            rows = pl.ds(pl.multiple_of(tw // W_STEP * WR, WR), WR)
+            for d, dev in ((2, at(x=xo)), (1, right), (3, left)):
+                send(w_out.at[d - 1, rows], w_in.at[d - 1, rows], s_w.at[d - 1], r_w.at[d - 1], dev)
+
+        @pl.when(slot < 4)
         def _():
             turn(slot)
 
-        @pl.when(slot < STEPS * CL * CL)
-        def _():
-            place(slot)
-
-    def wait_panel(s):
-        for k in range(PIECES):
-            drain(pan.at[s, xo, k * PC : k * PC + PH], r_br.at[s * PIECES + k])
-            drain(pan.at[s, xo, k * PC + PH : (k + 1) * PC], r_bl.at[s * PIECES + k])
-
-    def panel_rows(s, n):
-        lanes = slice(n * 256, (n + 1) * 256)
-        rows = jnp.dot(
-            dense[s], pan[s].reshape(CL * PAD, MODES)[:, lanes], preferred_element_type=F32
-        ).astype(BF)
-        for r in range(CL):
-            tsp[s, r * PAD : r * PAD + BS, lanes] = rows[r * BS : (r + 1) * BS]
+        @pl.when(slot < 8)
+        def _():
+            for i in range(2):
+                for s in range(STEPS):
+                    place(s, slot % CL, slot // CL * 2 + i)
+
+        for i, d in enumerate((2, 1, 3)):
+            @pl.when(slot == W_AT + i)
+            def _(d=d):
+                w_out[d - 1] = multiply((x + d) % X).astype(BF)
+
+        @pl.when(slot == W_AT + 3)
+        def _():
+            w_own[...] = multiply(x)
+
+        @pl.when(slot == W_SUM)
+        def _():
+            for d in range(X - 1):
+                drain(w_in.at[d], r_w.at[d])
+
+            @pl.loop(0, HM // 64)
+            def _(m):
+                for k in range(CORES):
+                    rows = pl.ds(pl.multiple_of(k * HM + m * 64, 64), 64)
+                    to = pl.ds(pl.multiple_of(m * 64, 64), 64)
+                    total = w_own[rows]
+                    for d in range(X - 1):
+                        total += w_in[d, rows].astype(F32)
+                    big = total.astype(BF)
+                    small = (total - big.astype(F32)).astype(BF)
+
+                    @pl.when(core == k)
+                    def _():
+                        w_sum[core, 0, to] = big
+                        w_sum[core, 1, to] = small
+
+                    @pl.when(core != k)
+                    def _():
+                        w_pass[0, to] = big
+                        w_pass[1, to] = small
+
+            send(w_pass, w_sum.at[core], s_c, r_c, other)
 
     def project(s, n):
-        part = jnp.dot(
-            basis_t[...], tsp[s, :, n * 256 : (n + 1) * 256], preferred_element_type=F32
-        ).reshape(COLS, CORES, 8, 256)
-        for k in range(CORES):
-            share[k, s, n] = part[:, k]
-        send(share.at[1 - core, s, n], core_in.at[s, n], s_core.at[s, n], r_core.at[s, n], at(core=1 - core))
+        cols = slice(s * 256, s * 256 + PAD)
+        part = jnp.zeros((HM, 256), F32)
+        for g in range(CORES):
+            panel = q[g, s, :, n * 256 : (n + 1) * 256]
+            for t in range(2):
+                part += jnp.dot(w_sum[g, t, :, cols], panel, preferred_element_type=F32)
+        part = part.reshape(COLS, 8, 256)
+        for i in range(X):
+            both = jnp.concatenate([part[zz * X + i] for zz in range(Z)], axis=0)
+
+            @pl.when(i == x)
+            def _():
+                for j in range(2):
+                    kept[s, n * 2 + j] = both[:, j * 128 : (j + 1) * 128]
+
+            both = both.astype(BF)
+            for j in range(2):
+                mine[s, i, n * 2 + j] = both[:, j * 128 : (j + 1) * 128]
 
     def over_plane(s):
-        for n in range(NH):
-            drain(core_in.at[s, n], r_core.at[s, n])
-            for i in range(X):
-                both = jnp.concatenate(
-                    [share[core, s, n, zz * X + i] + core_in[s, n, zz * X + i] for zz in range(Z)], axis=0
-                ).astype(BF)
-                for j in range(2):
-                    mine[s, i, n * 2 + j] = both[:, j * 128 : (j + 1) * 128]
         for i, (dx, dy) in enumerate(plane):
             xx, yy = (x + dx) % X, (y + dy) % Y
             send(mine.at[s, xx, yy], theirs.at[s, x, y], s_p.at[s, i], r_p.at[s, x * Y + y], at(x=xx, y=yy))
 
     def over_z():
         for s in range(STEPS):
-            total = mine[s, x, y].astype(F32)
+            total = kept[s, y]
             for dx, dy in plane:
                 xx, yy = (x + dx) % X, (y + dy) % Y
                 drain(theirs.at[s, xx, yy], r_p.at[s, xx * Y + yy])
@@ -302,18 +335,12 @@
                 for j in range(Y):
                     out[s, k * 8 : (k + 1) * 8, j * 128 : (j + 1) * 128] = out_all[s, j, k]
 
-    wait_panel(0)
-    panel_rows(0, 0)
-    panel_rows(0, 1)
-    project(0, 0)
-    project(0, 1)
-    wait_panel(1)
-    panel_rows(1, 0)
-    over_plane(0)
-    panel_rows(1, 1)
-    project(1, 0)
-    project(1, 1)
-    over_plane(1)
+    drain(w_sum.at[0], r_c)
+    for s in range(STEPS):
+        drain(up_in.at[s], r_q.at[s])
+        for n in range(NH):
+            project(s, n)
+        over_plane(s)
     over_z()
     spread()
     finish()
@@ -333,12 +360,11 @@
     def _():
         drain(dn_out, s_z.at[1])
 
-    for i in range(2):
-        drain(up_out, s_ag.at[i])
-        drain(up_out.at[0], s_fw.at[i])
+    for d in range(X - 1):
+        drain(w_out.at[d], s_w.at[d])
+    drain(w_pass, s_c)
+    drain(up_in, s_q)
     for s in range(STEPS):
-        for n in range(NH):
-            drain(core_in.at[s, n], s_core.at[s, n])
         for i in range(len(plane)):
             drain(mine.at[s, 0, 0], s_p.at[s, i])
     for d in range(RING - 1):
@@ -352,9 +378,13 @@
     vmem = pltpu.VMEM
     scratch = [
         vmem((STEPS * RUN, BS, BS), BF),
-        vmem((STEPS, CL * BS, CL * PAD), BF),
-        vmem((MODES, CL * PAD), BF),
-        vmem((STEPS, CL * PAD, MODES), BF),
+        vmem((CL, CL * BS, W2), BF),
+        vmem((MODES, CL * BS), BF),
+        vmem((MODES, W2), F32),
+        vmem((X - 1, MODES, W2), BF),
+        vmem((X - 1, MODES, W2), BF),
+        vmem((CORES, 2, HM, W2), BF),
+        vmem((2, HM, W2), BF),
         vmem((X, BS, MODES), BF),
         vmem((BS // 2, MODES), BF),
         vmem((BS // 2, MODES), BF),
@@ -362,19 +392,17 @@
         vmem((STEPS, BS, MODES), BF),
         vmem((STEPS, BS, MODES), BF),
         vmem((STEPS, BS, MODES), BF),
-        vmem((STEPS, CL, PAD, MODES), BF),
-        vmem((CORES, STEPS, NH, COLS, 8, 256), F32),
-        vmem((STEPS, NH, COLS, 8, 256), F32),
+        vmem((CORES, STEPS, PAD, MODES), BF),
         vmem((STEPS, X, Y, 8 * Z, 128), BF),
+        vmem((STEPS, Y, 8 * Z, 128), F32),
         vmem((STEPS, X, Y, 8 * Z, 128), BF),
         vmem((STEPS, Z, 8, 128), F32),
         vmem((RING, 8, 128), F32),
         vmem((STEPS, Y, CORES, 8, 128), F32),
-        dma, dma((2,)), dma((2,)), dma((2,)), dma((2,)), dma((2,)), dma((2,)),
-        dma((STEPS, NH)), dma((STEPS, X * Y - 1)), dma((RING - 1,)), dma((ZH * Y * CORES - 1,)),
+        dma, dma((2,)), dma((2,)), dma((2,)), dma((2,)), dma((X - 1,)), dma, dma,
+        dma((STEPS, X * Y - 1)), dma((RING - 1,)), dma((ZH * Y * CORES - 1,)),
         dma((PIECES,)), dma((PIECES,)), dma((PIECES,)), dma((PIECES,)), dma((PIECES,)), dma((PIECES,)),
-        dma((T,)), dma((T,)), dma((G,)), dma((G,)), dma((G,)), dma((G,)),
-        dma((STEPS, NH)), dma((STEPS, X * Y)), dma((RING,)), dma((ZH * Y * CORES,)),
+        dma((T,)), dma((T,)), dma((X - 1,)), dma, dma((STEPS,)), dma((STEPS, X * Y)), dma((RING,)), dma((ZH * Y * CORES,)),
     ]
     smem = pl.BlockSpec(memory_space=pltpu.SMEM)
     whole = pl.BlockSpec(memory_space=pltpu.VMEM)

time: 116 us -> 107 us (0.922)
  Pallas kernels: 115 us -> 105 us
    pallas_call x1, Pallas kernels: 115 us -> 105 us  [local(): pl.pallas_call(body, out_shape=jax.ShapeDtypeStruct((STEPS, CORES * 8, MO...]
where the time goes in v2:
time: 107 us
  Pallas kernels  105 us (98%)
  local copies, waits for them, and re-layouts  1.52 us (1%)
    pallas_call x1, Pallas kernels, local(): pl.pallas_call(body, out_shape=jax.ShapeDtypeStruct((STEPS, CORES * 8, MO...  105 us

profile of v2, /device:TPU:1, one launch (start us, length us, event | category | flops | bytes accessed | tf_op | source)
XLA Modules:
  0.0 106.6 jit_solution(10239821356164099759)
XLA Ops:
  0.0 105.1 %galerkin.1 = f32[2,16,512]{2,1,0:T(8,128)} custom-call(s32[2]{0:T(128)} %owner.1, s32[16]{0:T(128)} %brow.1, s32[16]{0:T(128)} %bcol.1, bf16[4,320,512]{2,1,0:T(8,128)(2,1)} %basis.1, bf16[16,320,320]{2,1,0:T(8,128)(2,1)} %blocks.1), custom_call_target="tpu_custom_call" | custom-call | flops 4000000000 | bytes 5000000 | tf_op jit(solution)/shard_map/galerkin/pallas_call | solution.py:409
  105.1 1.5 %copy.6 = f32[16,2,512]{2,1,0:T(2,128)} copy(f32[16,2,512]{2,0,1:T(8,128)} %bitcast.1) | data formatting | bytes 131072 | tf_op jit(solution)/shard_map/transpose | solution.py:421

commit v3 on v2

--- a/solution.py
+++ b/solution.py
@@ -17,15 +17,15 @@
 PH = PC // 2
 T = STEPS * CHUNKS
 G = STEPS * PIECES
-SKEW = 3
-AHEAD = 4
-LEAD = 3
+SKEW = 5
+AHEAD = 5
+LEAD = 5
 WP = 8
 WR = MODES // WP
 HM = MODES // CORES
 W_AT = 8
-W_GO, W_STEP = 11, 2
-W_SUM = 36
+W_GO, W_STEP = 11, 4
+W_SUM = 50
 COLS = X * Z
 NH = 2
 BF, F32 = jnp.bfloat16, jnp.float32
@@ -249,27 +249,30 @@
             for d in range(X - 1):
                 drain(w_in.at[d], r_w.at[d])
 
-            @pl.loop(0, HM // 64)
-            def _(m):
-                for k in range(CORES):
-                    rows = pl.ds(pl.multiple_of(k * HM + m * 64, 64), 64)
-                    to = pl.ds(pl.multiple_of(m * 64, 64), 64)
-                    total = w_own[rows]
-                    for d in range(X - 1):
-                        total += w_in[d, rows].astype(F32)
-                    big = total.astype(BF)
-                    small = (total - big.astype(F32)).astype(BF)
-
-                    @pl.when(core == k)
-                    def _():
-                        w_sum[core, 0, to] = big
-                        w_sum[core, 1, to] = small
-
-                    @pl.when(core != k)
-                    def _():
-                        w_pass[0, to] = big
-                        w_pass[1, to] = small
-
+        @pl.when((slot >= W_SUM) & (slot < W_SUM + HM // 64))
+        def _():
+            m = slot - W_SUM
+            to = pl.ds(pl.multiple_of(m * 64, 64), 64)
+            for k in range(CORES):
+                rows = pl.ds(pl.multiple_of(k * HM + m * 64, 64), 64)
+                total = w_own[rows]
+                for d in range(X - 1):
+                    total += w_in[d, rows].astype(F32)
+                big = total.astype(BF)
+                small = (total - big.astype(F32)).astype(BF)
+
+                @pl.when(core == k)
+                def _():
+                    w_sum[core, 0, to] = big
+                    w_sum[core, 1, to] = small
+
+                @pl.when(core != k)
+                def _():
+                    w_pass[0, to] = big
+                    w_pass[1, to] = small
+
+        @pl.when(slot == W_SUM + HM // 64 - 1)
+        def _():
             send(w_pass, w_sum.at[core], s_c, r_c, other)
 
     def project(s, n):

time: 107 us -> 103 us (0.963)
  Pallas kernels: 105 us -> 102 us
    pallas_call x1, Pallas kernels: 105 us -> 102 us  [local(): pl.pallas_call(body, out_shape=jax.ShapeDtypeStruct((STEPS, CORES * 8, MO...]
where the time goes in v3:
time: 103 us
  Pallas kernels  102 us (99%)
  local copies, waits for them, and re-layouts  1.52 us (1%)
    pallas_call x1, Pallas kernels, local(): pl.pallas_call(body, out_shape=jax.ShapeDtypeStruct((STEPS, CORES * 8, MO...  102 us

profile of v3, /device:TPU:1, one launch (start us, length us, event | category | flops | bytes accessed | tf_op | source)
XLA Modules:
  0.0 103.3 jit_solution(14688196229785512371)
XLA Ops:
  0.0 101.7 %galerkin.1 = f32[2,16,512]{2,1,0:T(8,128)} custom-call(s32[2]{0:T(128)} %owner.1, s32[16]{0:T(128)} %brow.1, s32[16]{0:T(128)} %bcol.1, bf16[4,320,512]{2,1,0:T(8,128)(2,1)} %basis.1, bf16[16,320,320]{2,1,0:T(8,128)(2,1)} %blocks.1), custom_call_target="tpu_custom_call" | custom-call | flops 4000000000 | bytes 5000000 | tf_op jit(solution)/shard_map/galerkin/pallas_call | solution.py:412
  101.7 1.5 %copy.6 = f32[16,2,512]{2,1,0:T(2,128)} copy(f32[16,2,512]{2,0,1:T(8,128)} %bitcast.1) | data formatting | bytes 131072 | tf_op jit(solution)/shard_map/transpose | solution.py:424

commit v4 on v3

--- a/solution.py
+++ b/solution.py
@@ -24,8 +24,9 @@
 WR = MODES // WP
 HM = MODES // CORES
 W_AT = 8
-W_GO, W_STEP = 11, 4
-W_SUM = 50
+W_GO, W_STEP = 11, 3
+W_SUM = 46
+EARLY = 56
 COLS = X * Z
 NH = 2
 BF, F32 = jnp.bfloat16, jnp.float32
@@ -62,11 +63,11 @@
     pltpu.make_async_copy(ref, ref, sem).wait()
 
 
-def meet(peers):
+def greet(peers):
     barrier = pltpu.get_barrier_semaphore()
     for dev in peers:
         pl.semaphore_signal(barrier, inc=1, device_id=dev, device_id_type=pl.DeviceIdType.MESH)
-    pl.semaphore_wait(barrier, len(peers))
+    return barrier
 
 
 def body(
@@ -97,7 +98,12 @@
         if dc or (dh and dy):
             hh, yy, cc = copy_at(dh, dy, dc)
             peers.append(at(zh=hh, y=yy, core=cc))
-    meet(peers)
+    barrier = greet(peers)
+    got[0] = basis[x]
+    for g in range(CORES):
+        q[g, 0, BS:] = jnp.zeros((PAD - BS, MODES), BF)
+        q[g, 1, : PAD - BS] = jnp.zeros((PAD - BS, MODES), BF)
+    pl.semaphore_wait(barrier, len(peers))
 
     def piece(k):
         start = k * PC
@@ -117,11 +123,6 @@
 
     for k in range(AHEAD):
         offer(k)
-    got[0] = basis[x]
-    for g in range(CORES):
-        q[g, 0, BS:] = jnp.zeros((PAD - BS, MODES), BF)
-        q[g, 1, : PAD - BS] = jnp.zeros((PAD - BS, MODES), BF)
-
     def turn(m):
         lanes = pl.ds(pl.multiple_of(m * 128, 128), 128)
         flipped = basis[:, :, lanes].reshape(CL * BS, 128).astype(F32).T.reshape(8, CORES, 8, CL * BS)
@@ -143,137 +144,6 @@
         return jnp.dot(basis_t[...], dense[c], preferred_element_type=F32)
 
     fetch.wait()
-
-    owner_x = [owner[s] % X for s in range(STEPS)]
-    owner_z = [owner[s] // X for s in range(STEPS)]
-    far = jnp.maximum(z, Z - 1 - z)
-
-    def pick(s, values):
-        return jnp.where(s == 0, values[0], values[1])
-
-    reach = LEAD + SKEW * far
-
-    @pl.loop(0, LEAD + SKEW * (Z - 1) + T)
-    def _(slot):
-        @pl.when(slot < PIECES)
-        def _():
-            rows, first, second, half = piece(slot)
-            drain(tr.at[half], r_tr.at[slot])
-            send(tr.at[half], got.at[2, first], s_rl.at[0], r_fr.at[slot], right)
-            drain(tl.at[half], r_tl.at[slot])
-            send(tl.at[half], got.at[2, second], s_rl.at[1], r_fl.at[slot], left)
-
-        @pl.when(slot < PIECES - AHEAD)
-        def _():
-            offer(slot + AHEAD)
-
-        tg = slot - LEAD
-        @pl.when((tg >= 0) & (tg < PIECES))
-        def _():
-            rows, first, second, half = piece(tg)
-            drain(got.at[3, rows], r_right.at[tg])
-            drain(got.at[1, rows], r_left.at[tg])
-            drain(got.at[2, first], r_fr.at[tg])
-            drain(got.at[2, second], r_fl.at[tg])
-
-        def stream(t, inn, outt, rsem, ssem, has_in, has_out, dev):
-            s, k = t // CHUNKS, t % CHUNKS
-            rows = pl.ds(pl.multiple_of(k * CH, CH), CH)
-            gap = (pick(s, owner_x) + X - x) % X
-            own = got[0, rows]
-            for d in range(1, X):
-                own = jnp.where(gap == d, got[d, rows], own)
-
-            @pl.when(has_in)
-            def _():
-                drain(inn.at[s, rows], rsem.at[t])
-                outt[s, rows] = jnp.where(pick(s, owner_z) == z, own, inn[s, rows])
-
-            @pl.when(jnp.logical_not(has_in))
-            def _():
-                outt[s, rows] = own
-
-            @pl.when(has_out)
-            def _():
-                send(outt.at[s, rows], inn.at[s, rows], ssem, rsem.at[t], dev)
-
-        tu = slot - LEAD - SKEW * z
-        @pl.when((tu >= 0) & (tu < T))
-        def _():
-            stream(tu, up_in, up_out, r_up, s_z.at[0], z > 0, z < Z - 1, above)
-
-        td = slot - LEAD - SKEW * (Z - 1 - z)
-        @pl.when((td >= 0) & (td < T))
-        def _():
-            stream(td, dn_in, dn_out, r_dn, s_z.at[1], z < Z - 1, z > 0, below)
-
-        tq = slot - reach
-        @pl.when((tq >= 0) & (tq < T))
-        def _():
-            s, k = tq // CHUNKS, tq % CHUNKS
-            rows = pl.ds(pl.multiple_of(k * CH, CH), CH)
-            here_rows = pl.ds(pl.multiple_of(s * (PAD - BS) + k * CH, CH), CH)
-            q[core, s, here_rows] = jnp.where(pick(s, owner_z) <= z, up_out[s, rows], dn_out[s, rows])
-
-
-            send(q.at[core, s, here_rows], q.at[core, s, here_rows], s_q, r_q.at[s], other)
-
-        tw = slot - W_GO
-        @pl.when((tw >= 0) & (tw % W_STEP == 0) & (tw < WP * W_STEP))
-        def _():
-            rows = pl.ds(pl.multiple_of(tw // W_STEP * WR, WR), WR)
-            for d, dev in ((2, at(x=xo)), (1, right), (3, left)):
-                send(w_out.at[d - 1, rows], w_in.at[d - 1, rows], s_w.at[d - 1], r_w.at[d - 1], dev)
-
-        @pl.when(slot < 4)
-        def _():
-            turn(slot)
-
-        @pl.when(slot < 8)
-        def _():
-            for i in range(2):
-                for s in range(STEPS):
-                    place(s, slot % CL, slot // CL * 2 + i)
-
-        for i, d in enumerate((2, 1, 3)):
-            @pl.when(slot == W_AT + i)
-            def _(d=d):
-                w_out[d - 1] = multiply((x + d) % X).astype(BF)
-
-        @pl.when(slot == W_AT + 3)
-        def _():
-            w_own[...] = multiply(x)
-
-        @pl.when(slot == W_SUM)
-        def _():
-            for d in range(X - 1):
-                drain(w_in.at[d], r_w.at[d])
-
-        @pl.when((slot >= W_SUM) & (slot < W_SUM + HM // 64))
-        def _():
-            m = slot - W_SUM
-            to = pl.ds(pl.multiple_of(m * 64, 64), 64)
-            for k in range(CORES):
-                rows = pl.ds(pl.multiple_of(k * HM + m * 64, 64), 64)
-                total = w_own[rows]
-                for d in range(X - 1):
-                    total += w_in[d, rows].astype(F32)
-                big = total.astype(BF)
-                small = (total - big.astype(F32)).astype(BF)
-
-                @pl.when(core == k)
-                def _():
-                    w_sum[core, 0, to] = big
-                    w_sum[core, 1, to] = small
-
-                @pl.when(core != k)
-                def _():
-                    w_pass[0, to] = big
-                    w_pass[1, to] = small
-
-        @pl.when(slot == W_SUM + HM // 64 - 1)
-        def _():
-            send(w_pass, w_sum.at[core], s_c, r_c, other)
 
     def project(s, n):
         cols = slice(s * 256, s * 256 + PAD)
@@ -299,6 +169,148 @@
         for i, (dx, dy) in enumerate(plane):
             xx, yy = (x + dx) % X, (y + dy) % Y
             send(mine.at[s, xx, yy], theirs.at[s, x, y], s_p.at[s, i], r_p.at[s, x * Y + y], at(x=xx, y=yy))
+
+    owner_x = [owner[s] % X for s in range(STEPS)]
+    owner_z = [owner[s] // X for s in range(STEPS)]
+    far = jnp.maximum(z, Z - 1 - z)
+
+    def pick(s, values):
+        return jnp.where(s == 0, values[0], values[1])
+
+    reach = LEAD + SKEW * far
+
+    @pl.loop(0, LEAD + SKEW * (Z - 1) + T)
+    def _(slot):
+        @pl.when(slot < PIECES)
+        def _():
+            rows, first, second, half = piece(slot)
+            drain(tr.at[half], r_tr.at[slot])
+            send(tr.at[half], got.at[2, first], s_rl.at[0], r_fr.at[slot], right)
+            drain(tl.at[half], r_tl.at[slot])
+            send(tl.at[half], got.at[2, second], s_rl.at[1], r_fl.at[slot], left)
+
+        @pl.when(slot < PIECES - AHEAD)
+        def _():
+            offer(slot + AHEAD)
+
+        tg = slot - LEAD
+        @pl.when((tg >= 0) & (tg < PIECES))
+        def _():
+            rows, first, second, half = piece(tg)
+            drain(got.at[3, rows], r_right.at[tg])
+            drain(got.at[1, rows], r_left.at[tg])
+            drain(got.at[2, first], r_fr.at[tg])
+            drain(got.at[2, second], r_fl.at[tg])
+
+        def stream(t, inn, outt, rsem, ssem, has_in, has_out, dev):
+            s, k = t // CHUNKS, t % CHUNKS
+            rows = pl.ds(pl.multiple_of(k * CH, CH), CH)
+            gap = (pick(s, owner_x) + X - x) % X
+            own = got[0, rows]
+            for d in range(1, X):
+                own = jnp.where(gap == d, got[d, rows], own)
+
+            @pl.when(has_in)
+            def _():
+                drain(inn.at[s, rows], rsem.at[t])
+                outt[s, rows] = jnp.where(pick(s, owner_z) == z, own, inn[s, rows])
+
+            @pl.when(jnp.logical_not(has_in))
+            def _():
+                outt[s, rows] = own
+
+            @pl.when(has_out)
+            def _():
+                send(outt.at[s, rows], inn.at[s, rows], ssem, rsem.at[t], dev)
+
+        tu = slot - LEAD - SKEW * z
+        @pl.when((tu >= 0) & (tu < T))
+        def _():
+            stream(tu, up_in, up_out, r_up, s_z.at[0], z > 0, z < Z - 1, above)
+
+        td = slot - LEAD - SKEW * (Z - 1 - z)
+        @pl.when((td >= 0) & (td < T))
+        def _():
+            stream(td, dn_in, dn_out, r_dn, s_z.at[1], z < Z - 1, z > 0, below)
+
+        tq = slot - reach
+        @pl.when((tq >= 0) & (tq < T))
+        def _():
+            s, k = tq // CHUNKS, tq % CHUNKS
+            rows = pl.ds(pl.multiple_of(k * CH, CH), CH)
+            here_rows = pl.ds(pl.multiple_of(s * (PAD - BS) + k * CH, CH), CH)
+            q[core, s, here_rows] = jnp.where(pick(s, owner_z) <= z, up_out[s, rows], dn_out[s, rows])
+
+
+            send(q.at[core, s, here_rows], q.at[core, s, here_rows], s_q, r_q.at[s], other)
+
+        tw = slot - W_GO
+        @pl.when((tw >= 0) & (tw % W_STEP == 0) & (tw < WP * W_STEP))
+        def _():
+            rows = pl.ds(pl.multiple_of(tw // W_STEP * WR, WR), WR)
+            for d, dev in ((2, at(x=xo)), (1, right), (3, left)):
+                send(w_out.at[d - 1, rows], w_in.at[d - 1, rows], s_w.at[d - 1], r_w.at[d - 1], dev)
+
+        @pl.when(slot < 4)
+        def _():
+            turn(slot)
+
+        @pl.when(slot < 8)
+        def _():
+            for i in range(2):
+                for s in range(STEPS):
+                    place(s, slot % CL, slot // CL * 2 + i)
+
+        for i, d in enumerate((2, 1, 3)):
+            @pl.when(slot == W_AT + i)
+            def _(d=d):
+                w_out[d - 1] = multiply((x + d) % X).astype(BF)
+
+        @pl.when(slot == W_AT + 3)
+        def _():
+            w_own[...] = multiply(x)
+
+        @pl.when(slot == W_SUM)
+        def _():
+            for d in range(X - 1):
+                drain(w_in.at[d], r_w.at[d])
+
+        @pl.when((slot >= W_SUM) & (slot < W_SUM + HM // 64))
+        def _():
+            m = slot - W_SUM
+            to = pl.ds(pl.multiple_of(m * 64, 64), 64)
+            for k in range(CORES):
+                rows = pl.ds(pl.multiple_of(k * HM + m * 64, 64), 64)
+                total = w_own[rows]
+                for d in range(X - 1):
+                    total += w_in[d, rows].astype(F32)
+                big = total.astype(BF)
+                small = (total - big.astype(F32)).astype(BF)
+
+                @pl.when(core == k)
+                def _():
+                    w_sum[core, 0, to] = big
+                    w_sum[core, 1, to] = small
+
+                @pl.when(core != k)
+                def _():
+                    w_pass[0, to] = big
+                    w_pass[1, to] = small
+
+        @pl.when(slot == W_SUM + HM // 64 - 1)
+        def _():
+            send(w_pass, w_sum.at[core], s_c, r_c, other)
+
+        @pl.when(slot == EARLY)
+        def _():
+            drain(w_sum.at[0], r_c)
+            drain(up_in.at[0], r_q.at[0])
+            project(0, 0)
+
+        @pl.when(slot == EARLY + 1)
+        def _():
+            project(0, 1)
+            over_plane(0)
 
     def over_z():
         for s in range(STEPS):
@@ -338,22 +350,16 @@
                 for j in range(Y):
                     out[s, k * 8 : (k + 1) * 8, j * 128 : (j + 1) * 128] = out_all[s, j, k]
 
-    drain(w_sum.at[0], r_c)
-    for s in range(STEPS):
-        drain(up_in.at[s], r_q.at[s])
-        for n in range(NH):
-            project(s, n)
-        over_plane(s)
-    over_z()
-    spread()
-    finish()
+    drain(up_in.at[1], r_q.at[1])
+    project(1, 0)
+    project(1, 1)
+    over_plane(1)
 
     drain(basis.at[xr], s_x.at[0])
     drain(basis.at[xl], s_x.at[1])
-    drain(tr, s_tr.at[0])
-    drain(tl, s_tr.at[1])
-    drain(tr, s_rl.at[0])
-    drain(tl, s_rl.at[1])
+    for i in range(2):
+        drain(tr, s_tr.at[i])
+        drain(tr, s_rl.at[i])
 
     @pl.when(z < Z - 1)
     def _():
@@ -367,11 +373,15 @@
         drain(w_out.at[d], s_w.at[d])
     drain(w_pass, s_c)
     drain(up_in, s_q)
+
+    over_z()
     for s in range(STEPS):
         for i in range(len(plane)):
             drain(mine.at[s, 0, 0], s_p.at[s, i])
+    spread()
     for d in range(RING - 1):
         drain(z_in.at[0], s_zz.at[d])
+    finish()
     for i in range(len(copies)):
         drain(z_in.at[0], s_out.at[i])
 

time: 103 us -> 105 us (1.019)
    pallas_call x1, Pallas kernels: 102 us -> 103 us  [local(): pl.pallas_call(body, out_shape=jax.ShapeDtypeStruct((STEPS, CORES * 8, MO...]
where the time goes in v4:
time: 105 us; the launch traced here: 104 us
  Pallas kernels  103 us (98%)
  local copies, waits for them, and re-layouts  1.52 us (1%)
    pallas_call x1, Pallas kernels, local(): pl.pallas_call(body, out_shape=jax.ShapeDtypeStruct((STEPS, CORES * 8, MO...  103 us

profile of v4, /device:TPU:1, one launch (start us, length us, event | category | flops | bytes accessed | tf_op | source)
XLA Modules:
  0.0 104.4 jit_solution(10512077452382238844)
XLA Ops:
  0.0 102.9 %galerkin.1 = f32[2,16,512]{2,1,0:T(8,128)} custom-call(s32[2]{0:T(128)} %owner.1, s32[16]{0:T(128)} %brow.1, s32[16]{0:T(128)} %bcol.1, bf16[4,320,512]{2,1,0:T(8,128)(2,1)} %basis.1, bf16[16,320,320]{2,1,0:T(8,128)(2,1)} %blocks.1), custom_call_target="tpu_custom_call" | custom-call | flops 4000000000 | bytes 5000000 | tf_op jit(solution)/shard_map/galerkin/pallas_call | solution.py:422
  102.9 1.5 %copy.6 = f32[16,2,512]{2,1,0:T(2,128)} copy(f32[16,2,512]{2,0,1:T(8,128)} %bitcast.1) | data formatting | bytes 131072 | tf_op jit(solution)/shard_map/transpose | solution.py:434

commit v5 on v4

--- a/solution.py
+++ b/solution.py
@@ -24,7 +24,8 @@
 WR = MODES // WP
 HM = MODES // CORES
 W_AT = 8
-W_GO, W_STEP = 11, 3
+WH = WR // 2
+W_GO, W_STEP, W_LAG = 11, 3, 5
 W_SUM = 46
 EARLY = 56
 COLS = X * Z
@@ -72,11 +73,11 @@
 
 def body(
     owner, brow, bcol, basis, blocks, out,
-    blk, dense, basis_t, w_own, w_out, w_in, w_sum, w_pass,
+    blk, dense, basis_t, w_own, w_out, w_tr, w_tl, w_in, w_sum, w_pass,
     got, tr, tl, up_in, dn_in, up_out, dn_out, q,
     mine, kept, theirs, b3, z_in, out_all,
     blk_sem, s_x, s_tr, s_rl, s_z, s_w, s_c, s_q, s_p, s_zz, s_out,
-    r_right, r_left, r_tr, r_tl, r_fr, r_fl, r_up, r_dn, r_w, r_c, r_q, r_p, r_zz, r_out,
+    r_right, r_left, r_tr, r_tl, r_fr, r_fl, r_up, r_dn, r_wtr, r_wtl, r_w, r_c, r_q, r_p, r_zz, r_out,
 ):
     here = Here()
     core, x, y, z, zh, zg, at, ring = here.core, here.x, here.y, here.z, here.zh, here.zg, here.at, here.ring
@@ -247,9 +248,25 @@
         tw = slot - W_GO
         @pl.when((tw >= 0) & (tw % W_STEP == 0) & (tw < WP * W_STEP))
         def _():
-            rows = pl.ds(pl.multiple_of(tw // W_STEP * WR, WR), WR)
-            for d, dev in ((2, at(x=xo)), (1, right), (3, left)):
-                send(w_out.at[d - 1, rows], w_in.at[d - 1, rows], s_w.at[d - 1], r_w.at[d - 1], dev)
+            k = tw // W_STEP
+            rows = pl.ds(pl.multiple_of(k * WR, WR), WR)
+            first = pl.ds(pl.multiple_of(k * WH, WH), WH)
+            second = pl.ds(pl.multiple_of(MODES // 2 + k * WH, WH), WH)
+            send(w_out.at[1, first], w_tr.at[first], s_w.at[0], r_wtr.at[k], right)
+            send(w_out.at[1, second], w_tl.at[first], s_w.at[1], r_wtl.at[k], left)
+            send(w_out.at[0, rows], w_in.at[0, rows], s_w.at[2], r_w.at[0], right)
+            send(w_out.at[2, rows], w_in.at[2, rows], s_w.at[3], r_w.at[1], left)
+
+        tv = slot - W_GO - W_LAG
+        @pl.when((tv >= 0) & (tv % W_STEP == 0) & (tv < WP * W_STEP))
+        def _():
+            k = tv // W_STEP
+            first = pl.ds(pl.multiple_of(k * WH, WH), WH)
+            second = pl.ds(pl.multiple_of(MODES // 2 + k * WH, WH), WH)
+            drain(w_tr.at[first], r_wtr.at[k])
+            send(w_tr.at[first], w_in.at[1, first], s_w.at[4], r_w.at[2], right)
+            drain(w_tl.at[first], r_wtl.at[k])
+            send(w_tl.at[first], w_in.at[1, second], s_w.at[5], r_w.at[3], left)
 
         @pl.when(slot < 4)
         def _():
@@ -272,8 +289,10 @@
 
         @pl.when(slot == W_SUM)
         def _():
-            for d in range(X - 1):
-                drain(w_in.at[d], r_w.at[d])
+            drain(w_in.at[0], r_w.at[0])
+            drain(w_in.at[2], r_w.at[1])
+            drain(w_in.at[1, : MODES // 2], r_w.at[2])
+            drain(w_in.at[1, MODES // 2 :], r_w.at[3])
 
         @pl.when((slot >= W_SUM) & (slot < W_SUM + HM // 64))
         def _():
@@ -369,8 +388,10 @@
     def _():
         drain(dn_out, s_z.at[1])
 
-    for d in range(X - 1):
-        drain(w_out.at[d], s_w.at[d])
+    for i in (0, 1, 4, 5):
+        drain(w_tr, s_w.at[i])
+    drain(w_out.at[0], s_w.at[2])
+    drain(w_out.at[2], s_w.at[3])
     drain(w_pass, s_c)
     drain(up_in, s_q)
 
@@ -395,6 +416,8 @@
         vmem((MODES, CL * BS), BF),
         vmem((MODES, W2), F32),
         vmem((X - 1, MODES, W2), BF),
+        vmem((MODES // 2, W2), BF),
+        vmem((MODES // 2, W2), BF),
         vmem((X - 1, MODES, W2), BF),
         vmem((CORES, 2, HM, W2), BF),
         vmem((2, HM, W2), BF),
@@ -412,10 +435,10 @@
         vmem((STEPS, Z, 8, 128), F32),
         vmem((RING, 8, 128), F32),
         vmem((STEPS, Y, CORES, 8, 128), F32),
-        dma, dma((2,)), dma((2,)), dma((2,)), dma((2,)), dma((X - 1,)), dma, dma,
+        dma, dma((2,)), dma((2,)), dma((2,)), dma((2,)), dma((6,)), dma, dma,
         dma((STEPS, X * Y - 1)), dma((RING - 1,)), dma((ZH * Y * CORES - 1,)),
         dma((PIECES,)), dma((PIECES,)), dma((PIECES,)), dma((PIECES,)), dma((PIECES,)), dma((PIECES,)),
-        dma((T,)), dma((T,)), dma((X - 1,)), dma, dma((STEPS,)), dma((STEPS, X * Y)), dma((RING,)), dma((ZH * Y * CORES,)),
+        dma((T,)), dma((T,)), dma((WP,)), dma((WP,)), dma((4,)), dma, dma((STEPS,)), dma((STEPS, X * Y)), dma((RING,)), dma((ZH * Y * CORES,)),
     ]
     smem = pl.BlockSpec(memory_space=pltpu.SMEM)
     whole = pl.BlockSpec(memory_space=pltpu.VMEM)

time: 105 us -> 109 us (1.038)
  Pallas kernels: 103 us -> 107 us
    pallas_call x1, Pallas kernels: 103 us -> 107 us  [local(): pl.pallas_call(body, out_shape=jax.ShapeDtypeStruct((STEPS, CORES * 8, MO...]
where the time goes in v5:
time: 109 us
  Pallas kernels  107 us (98%)
  local copies, waits for them, and re-layouts  1.52 us (1%)
    pallas_call x1, Pallas kernels, local(): pl.pallas_call(body, out_shape=jax.ShapeDtypeStruct((STEPS, CORES * 8, MO...  107 us

profile of v5, /device:TPU:1, one launch (start us, length us, event | category | flops | bytes accessed | tf_op | source)
XLA Modules:
  0.0 108.9 jit_solution(7309340965425743717)
XLA Ops:
  0.0 107.4 %galerkin.1 = f32[2,16,512]{2,1,0:T(8,128)} custom-call(s32[2]{0:T(128)} %owner.1, s32[16]{0:T(128)} %brow.1, s32[16]{0:T(128)} %bcol.1, bf16[4,320,512]{2,1,0:T(8,128)(2,1)} %basis.1, bf16[16,320,320]{2,1,0:T(8,128)(2,1)} %blocks.1), custom_call_target="tpu_custom_call" | custom-call | flops 4000000000 | bytes 5000000 | tf_op jit(solution)/shard_map/galerkin/pallas_call | solution.py:445
  107.4 1.5 %copy.6 = f32[16,2,512]{2,1,0:T(2,128)} copy(f32[16,2,512]{2,0,1:T(8,128)} %bitcast.1) | data formatting | bytes 131072 | tf_op jit(solution)/shard_map/transpose | solution.py:457

commit v6 on v4

--- a/solution.py
+++ b/solution.py
@@ -14,19 +14,17 @@
 CH = BS // CHUNKS
 PIECES = 10
 PC = BS // PIECES
-PH = PC // 2
 T = STEPS * CHUNKS
 G = STEPS * PIECES
-SKEW = 5
+SKEW = 4
 AHEAD = 5
-LEAD = 5
 WP = 8
 WR = MODES // WP
 HM = MODES // CORES
 W_AT = 8
-W_GO, W_STEP = 11, 3
-W_SUM = 46
-EARLY = 56
+W_GO = 11
+W_SUM = 38
+EARLY = 44
 COLS = X * Z
 NH = 2
 BF, F32 = jnp.bfloat16, jnp.float32
@@ -73,10 +71,10 @@
 def body(
     owner, brow, bcol, basis, blocks, out,
     blk, dense, basis_t, w_own, w_out, w_in, w_sum, w_pass,
-    got, tr, tl, up_in, dn_in, up_out, dn_out, q,
+    got, up_in, dn_in, up_out, dn_out, q,
     mine, kept, theirs, b3, z_in, out_all,
-    blk_sem, s_x, s_tr, s_rl, s_z, s_w, s_c, s_q, s_p, s_zz, s_out,
-    r_right, r_left, r_tr, r_tl, r_fr, r_fl, r_up, r_dn, r_w, r_c, r_q, r_p, r_zz, r_out,
+    blk_sem, s_x, s_z, s_w, s_c, s_q, s_p, s_zz, s_out,
+    r_x, r_up, r_dn, r_w, r_c, r_q, r_p, r_zz, r_out,
 ):
     here = Here()
     core, x, y, z, zh, zg, at, ring = here.core, here.x, here.y, here.z, here.zh, here.zg, here.at, here.ring
@@ -105,21 +103,10 @@
         q[g, 1, : PAD - BS] = jnp.zeros((PAD - BS, MODES), BF)
     pl.semaphore_wait(barrier, len(peers))
 
-    def piece(k):
-        start = k * PC
-        return (
-            pl.ds(pl.multiple_of(start, PC), PC),
-            pl.ds(pl.multiple_of(start, PH), PH),
-            pl.ds(pl.multiple_of(start + PH, PH), PH),
-            pl.ds(pl.multiple_of(k * PH, PH), PH),
-        )
-
     def offer(k):
-        rows, first, second, half = piece(k)
-        send(basis.at[xo, first], tr.at[half], s_tr.at[0], r_tr.at[k], right)
-        send(basis.at[xo, second], tl.at[half], s_tr.at[1], r_tl.at[k], left)
-        send(basis.at[xr, rows], got.at[3, rows], s_x.at[0], r_right.at[k], right)
-        send(basis.at[xl, rows], got.at[1, rows], s_x.at[1], r_left.at[k], left)
+        rows = pl.ds(pl.multiple_of(k * PC, PC), PC)
+        for d, dev in ((2, at(x=xo)), (1, right), (3, left)):
+            send(basis.at[(x + d) % X, rows], got.at[X - d, rows], s_x.at[d - 1], r_x.at[d - 1, k], dev)
 
     for k in range(AHEAD):
         offer(k)
@@ -177,30 +164,19 @@
     def pick(s, values):
         return jnp.where(s == 0, values[0], values[1])
 
-    reach = LEAD + SKEW * far
-
-    @pl.loop(0, LEAD + SKEW * (Z - 1) + T)
+    reach = SKEW * far
+
+    @pl.loop(0, SKEW * (Z - 1) + T)
     def _(slot):
+        @pl.when(slot < PIECES - AHEAD)
+        def _():
+            offer(slot + AHEAD)
+
         @pl.when(slot < PIECES)
         def _():
-            rows, first, second, half = piece(slot)
-            drain(tr.at[half], r_tr.at[slot])
-            send(tr.at[half], got.at[2, first], s_rl.at[0], r_fr.at[slot], right)
-            drain(tl.at[half], r_tl.at[slot])
-            send(tl.at[half], got.at[2, second], s_rl.at[1], r_fl.at[slot], left)
-
-        @pl.when(slot < PIECES - AHEAD)
-        def _():
-            offer(slot + AHEAD)
-
-        tg = slot - LEAD
-        @pl.when((tg >= 0) & (tg < PIECES))
-        def _():
-            rows, first, second, half = piece(tg)
-            drain(got.at[3, rows], r_right.at[tg])
-            drain(got.at[1, rows], r_left.at[tg])
-            drain(got.at[2, first], r_fr.at[tg])
-            drain(got.at[2, second], r_fl.at[tg])
+            rows = pl.ds(pl.multiple_of(slot * PC, PC), PC)
+            for d in range(1, X):
+                drain(got.at[X - d, rows], r_x.at[d - 1, slot])
 
         def stream(t, inn, outt, rsem, ssem, has_in, has_out, dev):
             s, k = t // CHUNKS, t % CHUNKS
@@ -223,12 +199,12 @@
             def _():
                 send(outt.at[s, rows], inn.at[s, rows], ssem, rsem.at[t], dev)
 
-        tu = slot - LEAD - SKEW * z
+        tu = slot - SKEW * z
         @pl.when((tu >= 0) & (tu < T))
         def _():
             stream(tu, up_in, up_out, r_up, s_z.at[0], z > 0, z < Z - 1, above)
 
-        td = slot - LEAD - SKEW * (Z - 1 - z)
+        td = slot - SKEW * (Z - 1 - z)
         @pl.when((td >= 0) & (td < T))
         def _():
             stream(td, dn_in, dn_out, r_dn, s_z.at[1], z < Z - 1, z > 0, below)
@@ -245,10 +221,10 @@
             send(q.at[core, s, here_rows], q.at[core, s, here_rows], s_q, r_q.at[s], other)
 
         tw = slot - W_GO
-        @pl.when((tw >= 0) & (tw % W_STEP == 0) & (tw < WP * W_STEP))
-        def _():
-            rows = pl.ds(pl.multiple_of(tw // W_STEP * WR, WR), WR)
-            for d, dev in ((2, at(x=xo)), (1, right), (3, left)):
+        for i, (d, dev) in enumerate(((2, at(x=xo)), (1, right), (3, left))):
+            @pl.when((tw >= 0) & (tw % (X - 1) == i) & (tw < WP * (X - 1)))
+            def _(d=d, dev=dev):
+                rows = pl.ds(pl.multiple_of(tw // (X - 1) * WR, WR), WR)
                 send(w_out.at[d - 1, rows], w_in.at[d - 1, rows], s_w.at[d - 1], r_w.at[d - 1], dev)
 
         @pl.when(slot < 4)
@@ -355,11 +331,8 @@
     project(1, 1)
     over_plane(1)
 
-    drain(basis.at[xr], s_x.at[0])
-    drain(basis.at[xl], s_x.at[1])
-    for i in range(2):
-        drain(tr, s_tr.at[i])
-        drain(tr, s_rl.at[i])
+    for d in range(X - 1):
+        drain(basis.at[d], s_x.at[d])
 
     @pl.when(z < Z - 1)
     def _():
@@ -399,8 +372,6 @@
         vmem((CORES, 2, HM, W2), BF),
         vmem((2, HM, W2), BF),
         vmem((X, BS, MODES), BF),
-        vmem((BS // 2, MODES), BF),
-        vmem((BS // 2, MODES), BF),
         vmem((STEPS, BS, MODES), BF),
         vmem((STEPS, BS, MODES), BF),
         vmem((STEPS, BS, MODES), BF),
@@ -412,9 +383,9 @@
         vmem((STEPS, Z, 8, 128), F32),
         vmem((RING, 8, 128), F32),
         vmem((STEPS, Y, CORES, 8, 128), F32),
-        dma, dma((2,)), dma((2,)), dma((2,)), dma((2,)), dma((X - 1,)), dma, dma,
+        dma, dma((X - 1,)), dma((2,)), dma((X - 1,)), dma, dma,
         dma((STEPS, X * Y - 1)), dma((RING - 1,)), dma((ZH * Y * CORES - 1,)),
-        dma((PIECES,)), dma((PIECES,)), dma((PIECES,)), dma((PIECES,)), dma((PIECES,)), dma((PIECES,)),
+        dma((X - 1, PIECES)),
         dma((T,)), dma((T,)), dma((X - 1,)), dma, dma((STEPS,)), dma((STEPS, X * Y)), dma((RING,)), dma((ZH * Y * CORES,)),
     ]
     smem = pl.BlockSpec(memory_space=pltpu.SMEM)

time: 105 us -> 107 us (1.019)
  Pallas kernels: 103 us -> 105 us
    pallas_call x1, Pallas kernels: 103 us -> 105 us  [local(): pl.pallas_call(body, out_shape=jax.ShapeDtypeStruct((STEPS, CORES * 8, MO...]
where the time goes in v6:
time: 107 us
  Pallas kernels  105 us (98%)
  local copies, waits for them, and re-layouts  1.52 us (1%)
    pallas_call x1, Pallas kernels, local(): pl.pallas_call(body, out_shape=jax.ShapeDtypeStruct((STEPS, CORES * 8, MO...  105 us

profile of v6, /device:TPU:1, one launch (start us, length us, event | category | flops | bytes accessed | tf_op | source)
XLA Modules:
  0.0 106.7 jit_solution(15400505605901948079)
XLA Ops:
  0.0 105.2 %galerkin.1 = f32[2,16,512]{2,1,0:T(8,128)} custom-call(s32[2]{0:T(128)} %owner.1, s32[16]{0:T(128)} %brow.1, s32[16]{0:T(128)} %bcol.1, bf16[4,320,512]{2,1,0:T(8,128)(2,1)} %basis.1, bf16[16,320,320]{2,1,0:T(8,128)(2,1)} %blocks.1), custom_call_target="tpu_custom_call" | custom-call | flops 4000000000 | bytes 5000000 | tf_op jit(solution)/shard_map/galerkin/pallas_call | solution.py:393
  105.2 1.5 %copy.6 = f32[16,2,512]{2,1,0:T(2,128)} copy(f32[16,2,512]{2,0,1:T(8,128)} %bitcast.1) | data formatting | bytes 131072 | tf_op jit(solution)/shard_map/transpose | solution.py:405

commit v7 on v5

--- a/solution.py
+++ b/solution.py
@@ -25,9 +25,8 @@
 HM = MODES // CORES
 W_AT = 8
 WH = WR // 2
-W_GO, W_STEP, W_LAG = 11, 3, 5
-W_SUM = 46
-EARLY = 56
+W_GO, W_STEP, W_LAG = 11, 3, 12
+W_SUM = 52
 COLS = X * Z
 NH = 2
 BF, F32 = jnp.bfloat16, jnp.float32
@@ -320,17 +319,6 @@
         def _():
             send(w_pass, w_sum.at[core], s_c, r_c, other)
 
-        @pl.when(slot == EARLY)
-        def _():
-            drain(w_sum.at[0], r_c)
-            drain(up_in.at[0], r_q.at[0])
-            project(0, 0)
-
-        @pl.when(slot == EARLY + 1)
-        def _():
-            project(0, 1)
-            over_plane(0)
-
     def over_z():
         for s in range(STEPS):
             total = kept[s, y]
@@ -369,6 +357,11 @@
                 for j in range(Y):
                     out[s, k * 8 : (k + 1) * 8, j * 128 : (j + 1) * 128] = out_all[s, j, k]
 
+    drain(w_sum.at[0], r_c)
+    drain(up_in.at[0], r_q.at[0])
+    project(0, 0)
+    project(0, 1)
+    over_plane(0)
     drain(up_in.at[1], r_q.at[1])
     project(1, 0)
     project(1, 1)

time: 109 us -> 104 us (0.954)
  Pallas kernels: 107 us -> 102 us
    pallas_call x1, Pallas kernels: 107 us -> 102 us  [local(): pl.pallas_call(body, out_shape=jax.ShapeDtypeStruct((STEPS, CORES * 8, MO...]
where the time goes in v7:
time: 104 us
  Pallas kernels  102 us (98%)
  local copies, waits for them, and re-layouts  1.52 us (1%)
    pallas_call x1, Pallas kernels, local(): pl.pallas_call(body, out_shape=jax.ShapeDtypeStruct((STEPS, CORES * 8, MO...  102 us

profile of v7, /device:TPU:1, one launch (start us, length us, event | category | flops | bytes accessed | tf_op | source)
XLA Modules:
  0.0 104.0 jit_solution(371631858697230712)
XLA Ops:
  0.0 102.4 %galerkin.1 = f32[2,16,512]{2,1,0:T(8,128)} custom-call(s32[2]{0:T(128)} %owner.1, s32[16]{0:T(128)} %brow.1, s32[16]{0:T(128)} %bcol.1, bf16[4,320,512]{2,1,0:T(8,128)(2,1)} %basis.1, bf16[16,320,320]{2,1,0:T(8,128)(2,1)} %blocks.1), custom_call_target="tpu_custom_call" | custom-call | flops 4000000000 | bytes 5000000 | tf_op jit(solution)/shard_map/galerkin/pallas_call | solution.py:438
  102.4 1.5 %copy.6 = f32[16,2,512]{2,1,0:T(2,128)} copy(f32[16,2,512]{2,0,1:T(8,128)} %bitcast.1) | data formatting | bytes 131072 | tf_op jit(solution)/shard_map/transpose | solution.py:450
